TPU v7x, 32 devices: a whole 2x2x4 slice. The times are simulated.
32 devices in a mesh: row: 4 (over z), col: 8 (over y, x, core).
Axes of the slice: x: 2, y: 2, z: 4, core: 2. Of those that a mesh axis runs over, the one named last changes fastest.
Arguments:
- front: float32 [16384, 16384], P('row', 'col')
- tiles: float32 [4096, 128, 128], P(('row', 'col')), may hold values from -0.375 to 0.375
- tile_block: int32 [2, 4096], replicated, may hold values from 0 to 127, as said below
- valid_rows: int32 [4096], P(('row', 'col')), may hold values from 64 to 128
Outputs:
- factored: float32 [16384, 16384], P('row', 'col')
Inputs may be any that keep to these rules, and one draw needn't show every extreme that they name: tile_block[0, t] and tile_block[1, t] give the block row and block column, in blocks of 128, that tile t is added to. The 128 tiles of each device (tiles laid in order over row+col) go to blocks held by exactly 16 different devices, 8 tiles to each.
All inputs are finite; a program needn't handle non-finite values.
Results may differ from a plain program's by a relative error of at most 0.0001.
Values sent between devices are 32-bit elements; how exact they have to be, the bound alone decides.
No kernel may reach another device: no remote copies, remote signals or barrier semaphores. Data moves between devices by JAX's collectives and lax.ppermute only.
A program may use at most 192 MiB of HBM per device.

v0:
```python
import functools

import jax
import jax.numpy as jnp
from jax import lax
from jax.experimental import pallas as pl
from jax.experimental.pallas import tpu as pltpu
from jax.sharding import PartitionSpec as P

NB = 128
PANELS = 2
TOTAL = NB * PANELS
MIB = 1 << 20
UNIT = 8


precise = lax.Precision.HIGHEST


def dot_nt(a, b, precision=precise):
    return lax.dot_general(
        a, b, (((1,), (1,)), ((), ())), precision=precision, preferred_element_type=jnp.float32
    )


def pack_kernel(slot_ref, valid_ref, tiles_ref, out_ref, buf, sem_in, sem_out):
    count, side = tiles_ref.shape[0], tiles_ref.shape[1]

    def fetch(t):
        return pltpu.make_async_copy(tiles_ref.at[t], buf.at[t], sem_in.at[t])

    def store(t):
        return pltpu.make_async_copy(buf.at[t], out_ref.at[jnp.maximum(slot_ref[t], 0)], sem_out.at[t])

    def each(act):
        @pl.loop(0, count)
        def _(t):
            @pl.when(slot_ref[t] >= 0)
            def _():
                act(t)

    def mask(t):
        fetch(t).wait()
        rows = lax.broadcasted_iota(jnp.int32, (side, side), 0)
        buf[t] = jnp.where(rows < valid_ref[t], buf[t], 0.0)
        store(t).start()

    each(lambda t: fetch(t).start())
    each(mask)
    each(lambda t: store(t).wait())


def pack(tiles, slots, valid, n_slots):
    count, side = tiles.shape[0], tiles.shape[1]
    smem = pl.BlockSpec(memory_space=pltpu.SMEM)
    return pl.pallas_call(
        pack_kernel,
        out_shape=jax.ShapeDtypeStruct((n_slots, side, side), jnp.float32),
        in_specs=[smem, smem, pl.BlockSpec(memory_space=pl.ANY)],
        out_specs=pl.BlockSpec(memory_space=pl.ANY),
        scratch_shapes=[
            pltpu.VMEM((count, side, side), jnp.float32),
            pltpu.SemaphoreType.DMA((count,)),
            pltpu.SemaphoreType.DMA((count,)),
        ],
        compiler_params=pltpu.CompilerParams(vmem_limit_bytes=24 * MIB),
    )(slots, valid, tiles)


def spread_kernel(
    width, stride, meta_ref, empty_ref, count_ref, tiles_ref, out_ref, code_ref, stage, sem
):
    count, units = tiles_ref.shape[0], tiles_ref.shape[1]
    devices, length = code_ref.shape

    @pl.loop(0, devices)
    def _(d):
        for k in range(length):
            code_ref[d, k] = -1

    @pl.loop(0, count)
    def _(i):
        tile, target, base = meta_ref[0, i], meta_ref[1, i], meta_ref[2, i]
        filled, code, valid = meta_ref[3, i], meta_ref[4, i], meta_ref[5, i]
        shape = tiles_ref.shape[1:]
        rows = lax.broadcasted_iota(jnp.int32, shape, 0) * shape[1]
        rows += lax.broadcasted_iota(jnp.int32, shape, 1)
        stage[target, pl.ds(base, units)] = jnp.where(rows < valid, tiles_ref[tile], 0.0)
        for u in range(units):
            code_ref[target, base + u] = jnp.where(u < filled, code + u * stride, -1)

    for half in range(2):
        first = 0 if half == 0 else count_ref[0]
        last = count_ref[0] if half == 0 else count
        free = count_ref[1 + half]

        def each_tile(i, carry):
            target, base, filled = meta_ref[1, i], meta_ref[2, i], meta_ref[3, i]

            def each_unit(q, carry):
                at, depth = carry
                relay = empty_ref[half, at]
                place = jnp.minimum(depth, width - 1)
                stage[relay, place] = stage[target, q]
                code_ref[relay, place] = code_ref[target, q]
                wrap = at + 1 >= free
                return jnp.where(wrap, 0, at + 1), jnp.where(wrap, depth + 1, depth)

            return lax.fori_loop(jnp.maximum(base, width), base + filled, each_unit, carry)

        lax.fori_loop(first, last, each_tile, (jnp.int32(0), jnp.int32(0)))

    copy = pltpu.make_async_copy(stage.at[:, pl.ds(0, width)], out_ref, sem)
    copy.start()
    copy.wait()


def spread(tiles, meta, empties, counts, devices, width, length, stride):
    count, side = tiles.shape[0], tiles.shape[1]
    units = side // UNIT
    smem = pl.BlockSpec(memory_space=pltpu.SMEM)
    return pl.pallas_call(
        functools.partial(spread_kernel, width, stride),
        out_shape=[
            jax.ShapeDtypeStruct((devices, width, UNIT, side), jnp.float32),
            jax.ShapeDtypeStruct((devices, length), jnp.int32),
        ],
        in_specs=[smem, smem, smem, pl.BlockSpec(memory_space=pltpu.VMEM)],
        out_specs=[pl.BlockSpec(memory_space=pl.ANY), smem],
        scratch_shapes=[
            pltpu.VMEM((devices, length, UNIT, side), jnp.float32),
            pltpu.SemaphoreType.DMA,
        ],
        compiler_params=pltpu.CompilerParams(vmem_limit_bytes=40 * MIB),
    )(meta, empties, counts, tiles.reshape(count, units, UNIT, side))


def relay_kernel(slot_ref, arrived_ref, out_ref):
    devices, width = slot_ref.shape

    @pl.loop(0, devices)
    def _(s):
        def more(k):
            return (k < width) & (slot_ref[s, jnp.minimum(k, width - 1)] >= 0)

        def move(k):
            out_ref[slot_ref[s, k]] = arrived_ref[s, k]
            return k + 1

        lax.while_loop(more, move, jnp.int32(0))


def relay(slots, arrived, length):
    vmem = pl.BlockSpec(memory_space=pltpu.VMEM)
    return pl.pallas_call(
        relay_kernel,
        out_shape=jax.ShapeDtypeStruct((length,) + arrived.shape[2:], jnp.float32),
        in_specs=[pl.BlockSpec(memory_space=pltpu.SMEM), vmem],
        out_specs=vmem,
        compiler_params=pltpu.CompilerParams(vmem_limit_bytes=40 * MIB),
    )(slots, arrived)


def add_kernel(
    cols_blocks, block_ref, unit_ref, index_ref, count_ref, partial_ref, arrived_ref, out_ref, buf,
    group_start, sem_in, sem_out
):
    slots, side = buf.shape[0], buf.shape[1]
    unit = arrived_ref.shape[1]
    ahead = slots // 2
    count = count_ref[0]

    def listed(i, carry):
        groups, last = carry
        block = block_ref[i]
        fresh = block != last

        @pl.when(fresh)
        def _():
            group_start[groups] = i

        return jnp.where(fresh, groups + 1, groups), block

    groups, _ = lax.fori_loop(0, count, listed, (jnp.int32(0), jnp.int32(-1)))
    group_start[groups] = count

    def window(g):
        block = block_ref[group_start[g]]
        rows = pl.ds(pl.multiple_of(block // cols_blocks * side, side), side)
        columns = pl.ds(pl.multiple_of(block % cols_blocks * side, side), side)
        return out_ref.at[rows, columns]

    def fetch(g):
        at = g % slots
        return pltpu.make_async_copy(window(g), buf.at[at], sem_in.at[at])

    def store(g):
        at = g % slots
        return pltpu.make_async_copy(buf.at[at], window(g), sem_out.at[at])

    @pl.loop(0, jnp.minimum(groups, ahead))
    def _(g):
        fetch(g).start()

    @pl.loop(0, groups)
    def _(g):
        @pl.when(g + ahead < groups)
        def _():
            @pl.when(g >= ahead)
            def _():
                store(g - ahead).wait()

            fetch(g + ahead).start()

        fetch(g).wait()

        @pl.loop(group_start[g], group_start[g + 1])
        def _(i):
            rows = pl.ds(pl.multiple_of(unit_ref[i] * unit, unit), unit)
            buf[g % slots, rows] += arrived_ref[index_ref[i]]

        store(g).start()

    @pl.loop(jnp.maximum(groups - slots, 0), groups)
    def _(g):
        store(g).wait()


def add_relayed(partial, arrived, listing, cols_blocks):
    row_len, col_len = partial.shape
    unit, side = arrived.shape[1:]
    smem = pl.BlockSpec(memory_space=pltpu.SMEM)
    hbm = pl.BlockSpec(memory_space=pl.ANY)
    return pl.pallas_call(
        functools.partial(add_kernel, cols_blocks),
        out_shape=jax.ShapeDtypeStruct((row_len, col_len), jnp.float32),
        in_specs=[smem, smem, smem, smem, hbm, pl.BlockSpec(memory_space=pltpu.VMEM)],
        out_specs=hbm,
        scratch_shapes=[
            pltpu.VMEM((16, side, side), jnp.float32),
            pltpu.SMEM((arrived.shape[0] + 1,), jnp.int32),
            pltpu.SemaphoreType.DMA((16,)),
            pltpu.SemaphoreType.DMA((16,)),
        ],
        input_output_aliases={4: 0},
        compiler_params=pltpu.CompilerParams(vmem_limit_bytes=24 * MIB),
    )(*listing, partial, arrived)


def panel_kernel(code_ref, first_ref, front_ref, arrived_ref, out_ref):
    side = arrived_ref.shape[1]

    @pl.when(first_ref[0] == 1)
    def _():
        out_ref[...] = front_ref[...]

    @pl.when(first_ref[0] == 0)
    def _():
        out_ref[...] = jnp.zeros_like(out_ref)

    @pl.loop(0, arrived_ref.shape[0])
    def _(k):
        code = code_ref[k]
        for part in range(PANELS):

            @pl.when((code >= 0) & (code % PANELS == part))
            def _():
                rows = pl.ds(pl.multiple_of(code // PANELS * side, side), side)
                out_ref[rows, part * side : (part + 1) * side] += arrived_ref[k]


def raw_panel(front, arrived, codes, first):
    row_len = front.shape[0]
    smem = pl.BlockSpec(memory_space=pltpu.SMEM)
    return pl.pallas_call(
        panel_kernel,
        grid=(1,),
        out_shape=jax.ShapeDtypeStruct((row_len, TOTAL), jnp.float32),
        in_specs=[
            smem,
            smem,
            pl.BlockSpec((row_len, TOTAL), lambda i: (0, 0)),
            pl.BlockSpec(arrived.shape, lambda i: (0, 0, 0)),
        ],
        out_specs=pl.BlockSpec((row_len, TOTAL), lambda i: (0, 0)),
        compiler_params=pltpu.CompilerParams(vmem_limit_bytes=40 * MIB),
    )(codes, first, front, arrived)


def split(value):
    high = value.astype(jnp.bfloat16)
    low = (value - high.astype(jnp.float32)).astype(jnp.bfloat16)
    return high, low


def rows_kernel(raw_ref, inverse_ref, out_ref, parts_ref):
    solved = dot_nt(raw_ref[...], inverse_ref[...])
    out_ref[...] = solved
    high, low = split(solved)
    parts_ref[:, :TOTAL] = high
    parts_ref[:, TOTAL : 2 * TOTAL] = high
    parts_ref[:, 2 * TOTAL :] = low


def solve_rows(raw, inverse):
    length = raw.shape[0]
    step = min(512, length)
    block = pl.BlockSpec((step, TOTAL), lambda i: (i, 0))
    return pl.pallas_call(
        rows_kernel,
        grid=(length // step,),
        out_shape=[
            jax.ShapeDtypeStruct((length, TOTAL), jnp.float32),
            jax.ShapeDtypeStruct((length, 3 * TOTAL), jnp.bfloat16),
        ],
        in_specs=[block, pl.BlockSpec((TOTAL, TOTAL), lambda i: (0, 0))],
        out_specs=[block, pl.BlockSpec((step, 3 * TOTAL), lambda i: (i, 0))],
        compiler_params=pltpu.CompilerParams(vmem_limit_bytes=24 * MIB),
    )(raw, inverse)


def cols_kernel(order_ref, raw_ref, inverse_ref, out_ref, parts_ref):
    solved = dot_nt(inverse_ref[...], raw_ref[0])
    out_ref[...] = solved
    high, low = split(solved)
    parts_ref[:TOTAL] = high
    parts_ref[TOTAL : 2 * TOTAL] = low
    parts_ref[2 * TOTAL :] = high


def solve_cols(chunks, order, inverse):
    count, step = chunks.shape[:2]
    length = count * step
    grid_spec = pltpu.PrefetchScalarGridSpec(
        num_scalar_prefetch=1,
        grid=(count,),
        in_specs=[
            pl.BlockSpec((1, step, TOTAL), lambda i, order: (order[i], 0, 0)),
            pl.BlockSpec((TOTAL, TOTAL), lambda i, order: (0, 0)),
        ],
        out_specs=[
            pl.BlockSpec((TOTAL, step), lambda i, order: (0, i)),
            pl.BlockSpec((3 * TOTAL, step), lambda i, order: (0, i)),
        ],
    )
    return pl.pallas_call(
        cols_kernel,
        grid_spec=grid_spec,
        out_shape=[
            jax.ShapeDtypeStruct((TOTAL, length), jnp.float32),
            jax.ShapeDtypeStruct((3 * TOTAL, length), jnp.bfloat16),
        ],
        compiler_params=pltpu.CompilerParams(vmem_limit_bytes=24 * MIB),
    )(order, chunks, inverse)


def final_kernel(
    cols_blocks, runs, code_ref, run_ref, place_ref, front_ref, rows_ref, rows_parts, cols_ref, cols_parts,
    lower_ref, arrived_ref, out_ref, cursor
):
    step = pl.program_id(0)
    sources, capacity = code_ref.shape
    height, width = front_ref.shape
    unit, side = arrived_ref.shape[2:]
    per_step = height // unit

    @pl.when(step == 0)
    def _():
        for s in range(sources):
            cursor[s] = 0

    chunk = min(512, width)
    for start in range(0, width, chunk):
        at = slice(start, start + chunk)
        change = jnp.dot(rows_parts[...], cols_parts[:, at], preferred_element_type=jnp.float32)
        out_ref[:, at] = front_ref[:, at] - change

    edge = (step + 1) * per_step * cols_blocks

    @pl.loop(0, sources)
    def _(s):
        def more(k):
            code = code_ref[s, jnp.minimum(k, capacity - 1)]
            return (k < capacity) & (code >= 0) & (code < edge)

        def add(k):
            code = code_ref[s, k]
            length = run_ref[s, k]
            unit_row = code // cols_blocks - step * per_step
            columns = pl.ds(pl.multiple_of(code % cols_blocks * side, side), side)
            for run in runs:
                skipped = length // (2 * run) * (2 * run)

                @pl.when(length // run % 2 == 1)
                def _():
                    rows = pl.ds(pl.multiple_of((unit_row + skipped) * unit, unit), run * unit)
                    block = arrived_ref[s, pl.ds(k + skipped, run)]
                    out_ref[rows, columns] += block.reshape(run * unit, side)

            return k + length

        cursor[s] = lax.while_loop(more, add, cursor[s])

    top = (place_ref[0] == 0) & (step == 0)

    @pl.when(top)
    def _():
        out_ref[...] = cols_ref[...]

    @pl.when(place_ref[1] == 0)
    def _():
        out_ref[:, :TOTAL] = jnp.where(top, lower_ref[...], rows_ref[...])


def finish(front, rows, cols, lower, arrived, codes, lengths, place, cols_blocks):
    row_len, col_len = front.shape
    height = TOTAL
    smem = pl.BlockSpec(memory_space=pltpu.SMEM)
    block = pl.BlockSpec((height, TOTAL), lambda i: (i, 0))
    parts = pl.BlockSpec((height, 3 * TOTAL), lambda i: (i, 0))
    wide = pl.BlockSpec((height, col_len), lambda i: (i, 0))
    whole = pl.BlockSpec((TOTAL, col_len), lambda i: (0, 0))
    whole_parts = pl.BlockSpec((3 * TOTAL, col_len), lambda i: (0, 0))
    runs = (16, 8, 4, 2, 1) if arrived.shape[2] == UNIT else (1,)
    return pl.pallas_call(
        functools.partial(final_kernel, cols_blocks, runs),
        grid=(row_len // height,),
        out_shape=jax.ShapeDtypeStruct((row_len, col_len), jnp.float32),
        in_specs=[
            smem, smem, smem, wide, block, parts, whole, whole_parts,
            pl.BlockSpec((TOTAL, TOTAL), lambda i: (0, 0)),
            pl.BlockSpec(memory_space=pltpu.VMEM),
        ],
        out_specs=wide,
        scratch_shapes=[pltpu.SMEM((codes.shape[0],), jnp.int32)],
        compiler_params=pltpu.CompilerParams(vmem_limit_bytes=56 * MIB),
    )(codes, lengths, place, front, *rows, *cols, lower, arrived)


def factor(diagonal):
    def lower_of(block):
        return jnp.linalg.cholesky(jnp.tril(block) + jnp.tril(block, -1).T)

    def inverse_of(block):
        return jax.scipy.linalg.solve_triangular(block, jnp.eye(NB, dtype=jnp.float32), lower=True)

    first = lower_of(diagonal[:NB, :NB])
    first_inverse = inverse_of(first)
    below = dot_nt(diagonal[NB:, :NB], first_inverse)
    second = lower_of(diagonal[NB:, NB:] - dot_nt(below, below))
    second_inverse = inverse_of(second)
    corner = -jnp.dot(second_inverse, jnp.dot(below, first_inverse, precision=precise), precision=precise)
    zero = jnp.zeros((NB, NB), jnp.float32)
    return jnp.block([[first, zero], [below, second]]), jnp.block([[first_inverse, zero], [corner, second_inverse]])


def body(front, tiles, tile_block, valid_rows):
    row_len, col_len = front.shape
    row_count = lax.axis_size("row")
    col_count = lax.axis_size("col")
    device_count = row_count * col_count
    per_device = tiles.shape[0]
    side = tiles.shape[1]
    capacity = 2 * per_device // device_count
    rows_blocks = row_len // side
    cols_blocks = col_len // side
    row_now = lax.axis_index("row")
    col_now = lax.axis_index("col")
    device_now = row_now * col_count + col_now

    block_row = tile_block[0].reshape(device_count, per_device)
    block_col = tile_block[1].reshape(device_count, per_device)
    target_row = block_row // rows_blocks
    target = target_row * col_count + block_col // cols_blocks
    code = block_row % rows_blocks * cols_blocks + block_col % cols_blocks
    position = lax.broadcasted_iota(jnp.int32, target.shape, 1)
    place = jnp.stack([row_now, col_now]).astype(jnp.int32)

    def own(values):
        return lax.dynamic_index_in_dim(values, device_now, 0, keepdims=False)

    in_panel = block_col < PANELS
    panel_key = jnp.where(in_panel, target_row, -1)
    panel_rank = jnp.sum(
        (panel_key[:, :, None] == panel_key[:, None, :]) & (position[:, None, :] < position[:, :, None]),
        axis=2,
    )
    same_col = lax.dynamic_index_in_dim(
        jnp.stack([panel_key, panel_rank, code]).reshape(3, row_count, col_count, per_device),
        col_now, 2, keepdims=False,
    )

    def send_panel(tiles, valid_rows, depth):
        ahead = (own(target_row) - row_now) % row_count
        fits = own(in_panel) & (own(panel_rank) < depth)
        panel_slot = jnp.where(fits, ahead * depth + own(panel_rank), -1)
        panel_out = pack(tiles, panel_slot, valid_rows, row_count * depth)
        panel_in = [panel_out[:depth]]
        for shift in range(1, row_count):
            sending = panel_out[shift * depth : (shift + 1) * depth]
            turn = [(r, (r + shift) % row_count) for r in range(row_count)]
            panel_in.append(lax.ppermute(sending, "row", turn))
        return panel_in

    def sum_panel(front, panel_in, depth):
        fits = (same_col[0] == row_now)[:, :, None] & (same_col[1][:, :, None] == jnp.arange(depth))
        panel_code = same_col[2] // cols_blocks * PANELS + same_col[2] % cols_blocks
        panel_codes = jnp.sum(jnp.where(fits, panel_code[:, :, None] + 1, 0), axis=1) - 1
        by_shift = (row_now - jnp.arange(row_count)) % row_count
        panel_codes = jnp.take(panel_codes, by_shift, axis=0).reshape(-1)
        first = (col_now == 0).astype(jnp.int32).reshape(1)
        return raw_panel(front, jnp.concatenate(panel_in, 0), panel_codes, first)

    def gather_panel(partial):
        chunk = lax.psum_scatter(partial, "col", scatter_dimension=0, tiled=True)
        raw_rows = lax.all_gather(chunk, "col", axis=0, tiled=True)
        chunk, raw_rows = lax.optimization_barrier((chunk, raw_rows))
        return lax.all_gather(chunk, "row", axis=0), raw_rows

    panel_depth = (capacity * 5 + 7) // 8
    panel_in = send_panel(tiles, valid_rows, panel_depth)

    units = side // UNIT
    length = capacity * units
    width = length * 41 // 64
    pass_on = length * 13 // 32
    half_count = device_count // 2
    half_base = device_now // half_count * half_count
    unit_rows = rows_blocks * units
    local_codes = unit_rows * cols_blocks
    own_target, own_code = own(target), own(code)
    own_position = own(position)
    filled = (valid_rows + UNIT - 1) // UNIT
    key = (own_target * rows_blocks * cols_blocks + own_code) * per_device + own_position
    before = key[None, :] < key[:, None]
    together = own_target[None, :] == own_target[:, None]
    base = jnp.sum(jnp.where(before & together, filled[None, :], 0), axis=1)
    order = jnp.sum(before, axis=1)
    unit_code = (own_target * unit_rows + own_code // cols_blocks * units) * cols_blocks
    unit_code += own_code % cols_blocks
    meta = jnp.stack([own_position, own_target, base, filled, unit_code, valid_rows])
    meta = jnp.sum(
        jnp.where(order[None, :, None] == jnp.arange(per_device), meta[:, :, None], 0), axis=1
    )
    to_device = own_target[:, None] == jnp.arange(device_count)
    load = jnp.sum(jnp.where(to_device, filled[:, None], 0), axis=0).reshape(2, half_count)
    empty = load == 0
    empty_rank = jnp.cumsum(empty, axis=1) - 1
    device_ids = jnp.arange(device_count).reshape(2, half_count)
    listed = (empty[:, :, None]) & (empty_rank[:, :, None] == jnp.arange(half_count))
    empties = jnp.sum(jnp.where(listed, device_ids[:, :, None], 0), axis=1)
    free = jnp.sum(empty, axis=1)
    left = jnp.sum(jnp.maximum(load - width, 0), axis=1)
    failed = jnp.any(left > free * width) | jnp.any(own(in_panel) & (own(panel_rank) >= panel_depth))
    counts = jnp.concatenate([jnp.sum(own_target < half_count)[None], free]).astype(jnp.int32)
    outgoing, sent_codes = spread(
        tiles, meta.astype(jnp.int32), empties.astype(jnp.int32), counts,
        device_count, width, length, cols_blocks,
    )

    partial = sum_panel(front, panel_in, panel_depth)
    partial, sent_codes = lax.optimization_barrier((partial, sent_codes))
    gathered, raw_rows = gather_panel(partial)
    got = lax.all_to_all(sent_codes[:, :width], ("row", "col"), 0, 0, tiled=True)
    outgoing, got = lax.optimization_barrier((outgoing, got))
    arrived = lax.all_to_all(outgoing, ("row", "col"), 0, 0, tiled=True)
    got_target = got // local_codes
    local = got % local_codes
    mine = (got >= 0) & (got_target == device_now)
    direct_codes = jnp.where(mine, local, -1)
    steps = jnp.arange(width)
    opening = (local // cols_blocks % units == 0) | jnp.logical_not(mine)
    later = (steps[None, :] > steps[:, None]) & opening[:, None, :]
    direct_runs = jnp.min(jnp.where(later, steps, width), axis=2) - steps
    total_units = device_count * width
    passing = ((got >= 0) & (got_target != device_now)).reshape(-1)
    flat_key = jnp.where(passing, got.reshape(-1) * total_units + jnp.arange(total_units), -1)
    flat_target = jnp.where(passing, got_target.reshape(-1), -1)
    rank = jnp.sum(
        (flat_target[None, :] == flat_target[:, None]) & (flat_key[None, :] < flat_key[:, None]), axis=1
    )
    failed = failed | jnp.any(passing & (rank >= pass_on))
    relay_slot = jnp.where(
        passing & (rank < pass_on), (flat_target - half_base) * pass_on + rank, -1
    )
    picked = relay_slot[:, None] == jnp.arange(half_count * pass_on)
    relay_codes = jnp.sum(jnp.where(picked, local.reshape(-1)[:, None] + 1, 0), axis=0) - 1
    notes = jnp.zeros((2, half_count, pass_on + 1), jnp.int32)
    notes = lax.dynamic_update_slice(
        notes, relay_codes.reshape(1, half_count, pass_on).astype(jnp.int32), (device_now // half_count, 0, 0)
    )
    notes = notes.at[:, :, pass_on].set(failed.astype(jnp.int32))
    def chain(gathered, raw_rows):
        diagonal = jnp.where(row_now == 0, raw_rows[:TOTAL], jnp.eye(TOTAL, dtype=jnp.float32))
        lower, inverse = factor(diagonal)
        known = jnp.where(row_now == 0, inverse, 0.0)
        gathered, known = lax.optimization_barrier((gathered, known))
        share = col_count // row_count
        chunks = []
        for turn in range(row_count):
            pairs = [
                (h * row_count + i, (i + turn) % row_count * share + h)
                for h in range(share)
                for i in range(row_count)
            ]
            sending = lax.dynamic_index_in_dim(gathered, (col_now + turn) % row_count, 0, keepdims=False)
            chunks.append(lax.ppermute(sending, "col", pairs))
        order = (col_now // share - jnp.arange(row_count)) % row_count
        inverse = known
        for other in range(1, row_count):
            inverse += lax.ppermute(known, "row", [(0, other)])
        return known, inverse, jnp.stack(chunks), order.astype(jnp.int32), lower

    def solve(raw_rows, inverse, chunks, order):
        rows = solve_rows(raw_rows, inverse)
        return rows, solve_cols(chunks, order, inverse)

    known, inverse, chunks, order, lower = chain(gathered, raw_rows)
    notes, arrived, known = lax.optimization_barrier((notes, arrived, known))
    notes = lax.all_to_all(
        notes.reshape(device_count, pass_on + 1), ("row", "col"), 0, 0, tiled=True
    )
    relay_codes = lax.dynamic_slice_in_dim(notes, half_base, half_count, 0)[:, :pass_on]
    relay_slot = relay_slot.reshape(device_count, width)

    flat = relay_codes.reshape(-1)
    unit_row, relay_col = flat // cols_blocks, flat % cols_blocks
    wanted = (flat >= 0) & ((row_now > 0) | (unit_row >= TOTAL // UNIT))
    wanted &= (col_now > 0) | (relay_col >= PANELS)
    relay_block = unit_row // units * cols_blocks + relay_col
    relay_key = jnp.where(wanted, relay_block * units + unit_row % units, local_codes)
    relay_key = relay_key * flat.shape[0] + jnp.arange(flat.shape[0])
    relay_order = jnp.sum(relay_key[None, :] < relay_key[:, None], axis=1)
    listing = jnp.stack([relay_block, unit_row % units, jnp.arange(flat.shape[0])])
    at_order = relay_order[None, :, None] == jnp.arange(flat.shape[0])
    listing = jnp.sum(jnp.where(at_order, listing[:, :, None], 0), axis=1).astype(jnp.int32)
    listing = [*listing, jnp.sum(wanted).astype(jnp.int32).reshape(1)]

    passed = relay(relay_slot, arrived, half_count * pass_on)
    passed, notes, inverse, chunks = lax.optimization_barrier((passed, notes, inverse, chunks))
    rows, cols = solve(raw_rows, inverse, chunks, order)
    too_full = jnp.any(notes[:, pass_on] != 0)
    halves = [list(range(half_count)), list(range(half_count, device_count))]
    passed = lax.all_to_all(
        passed.reshape(half_count, pass_on, UNIT, side), ("row", "col"), 0, 0,
        axis_index_groups=halves, tiled=True,
    )
    partial = finish(front, rows, cols, lower, arrived, direct_codes, direct_runs, place, cols_blocks)
    result = add_relayed(partial, passed.reshape(-1, UNIT, side), listing, cols_blocks)

    def padded():
        partial = sum_panel(front, send_panel(tiles, valid_rows, capacity), capacity)
        gathered, raw_rows = gather_panel(partial)
        order = (target * rows_blocks * cols_blocks + code) * per_device + position
        ranking = jnp.sum(
            (target[:, :, None] == target[:, None, :]) & (order[:, None, :] < order[:, :, None]), axis=2
        )
        slot = own(target) * capacity + own(ranking)
        here = (target == device_now)[:, :, None] & (ranking[:, :, None] == jnp.arange(capacity))
        codes = jnp.sum(jnp.where(here, code[:, :, None] + 1, 0), axis=1) - 1
        packed = pack(tiles, slot, valid_rows, device_count * capacity)
        arrived = lax.all_to_all(
            packed.reshape(device_count, capacity, side, side), ("row", "col"), 0, 0, tiled=True
        )
        _, inverse, chunks, order, lower = chain(gathered, raw_rows)
        rows, cols = solve(raw_rows, inverse, chunks, order)
        return finish(
            front, rows, cols, lower, arrived, codes, jnp.ones_like(codes), place, cols_blocks
        )

    def unfinished(state):
        return state[0] > 0

    def redo(state):
        return jnp.int32(0), padded()

    return lax.while_loop(unfinished, redo, (too_full.astype(jnp.int32), result))[1]


def solution(mesh):
    placed = (P("row", "col"), P(("row", "col"), None, None), P(), P(("row", "col")))
    return jax.shard_map(
        body, mesh=mesh, in_specs=placed, out_specs=P("row", "col"), check_vma=False
    )
```

profile of v0, /device:TPU:5, one launch (start us, length us, event | category | flops | bytes accessed | tf_op | source)
XLA Modules:
  0.0 499.7 jit_solution(10730052716482558350)
XLA Ops:
  10.6 6.9 %shard_map.47 = f32[20,128,128]{2,1,0:T(8,128)S(1)} custom-call(s32[128]{0:T(128)S(1)} %get-tuple-element.273.slot_ref, s32[128]{0:T(128)} %valid_ref.1, f32[128,128,128]{2,1,0:T(8,128)} %tiles_ref.1), custom_call_target="tpu_custom_call" | custom-call | tf_op jit(solution)/shard_map/pallas_call | solution.py:56
  17.7 4.0 collective-permute-start.12
  25.2 21.1 %shard_map.46 = (f32[32,82,8,128]{3,2,1,0:T(8,128)S(1)}, s32[32,128]{1,0:T(8,128)S(1)}) custom-call(s32[6,128]{1,0:T(8,128)S(1)} %select_reduce_fusion.7.meta_ref, s32[2,16]{1,0:T(2,128)S(1)} %select_reduce_fusion.11.empty_ref, s32[3]{0:T(128)S(1)} %pad_add_fusion.1.count_ref, f32[128,16,8,128]{3,2,1,0:T(8,128)} %bitcast.182), custom_call_target="tpu_custom_call" | custom-call | tf_op jit(solution)/shard_map/pallas_call | solution.py:122
  46.3 4.2 copy-done.9
  50.6 3.0 shard_map.48
  55.7 11.3 %all_to_all.39 = s32[32,1,82]{2,1,0:T(1,128)S(1)} all-to-all(s32[32,1,82]{2,1,0:T(1,128)S(1)} %bitcast.181), channel_id=1, replica_groups=mesh['row'=4,'col'=8] {'row','col'}, dimensions={0} | all-to-all | bytes 20992 | tf_op jit(solution)/shard_map/all_to_all | solution.py:564
  67.0 5.1 %all-to-all-start.2 = ((f32[32,82,8,128]{3,2,1,0:T(8,128)}), f32[32,82,8,128]{3,2,1,0:T(8,128)}, u32[]{:S(2)}, u32[]{:S(2)}) async-start(f32[32,82,8,128]{3,2,1,0:T(8,128)} %copy-done.9), calls=%async_computation.3 | async-start | bytes 21495808 | tf_op jit(solution)/shard_map/all_to_all | solution.py:566
  72.1 5.6 %copy.218 = f32[4096,256]{0,1:T(8,128)} copy(f32[4096,256]{1,0:T(8,128)} %copy-done.8) | data formatting | bytes 8388608 | tf_op jit(solution)/shard_map/optimization_barrier | solution.py:562
  77.8 118.3 %reduce-scatter.3.cloned.1.call-done = f32[512,256]{0,1:T(8,128)} async-done(((f32[4096,256]{0,1:T(8,128)}), f32[512,256]{0,1:T(8,128)}) %reduce-scatter.3.cloned.1.call-update) | async-done | bytes 524304 | tf_op jit(solution)/shard_map/reduce_scatter | solution.py:515
  201.9 6.2 %convert_reduce_fusion.1 = s32[2624]{0:T(1024)S(1)} fusion(s32[2624]{0:T(1024)S(1)} %get-tuple-element.272, s32[2624]{0:T(1024)S(1)} %get-tuple-element.271), kind=kLoop, calls=%fused_computation.99 | loop fusion | flops 34424256 | bytes 31488 | tf_op jit(solution)/shard_map/reduce_sum | solution.py:579
  209.2 45.7 %all-gather.8.cloned.1.call-done = f32[4096,256]{0,1:T(8,128)} async-done(((f32[512,256]{0,1:T(8,128)}), f32[4096,256]{0,1:T(8,128)}) %all-gather.8.cloned.1.call-update) | async-done | bytes 4194320 | tf_op jit(solution)/shard_map/all_gather | solution.py:516
  256.3 11.7 %custom-call.16 = f32[128,128]{1,0:T(8,128)S(1)} custom-call(f32[128,128]{1,0:T(8,128)S(1)} %copy.223), custom_call_target="Cholesky" | custom-call | tf_op jit(solution)/shard_map/jit(cholesky)/cholesky/custom-call.1 | solution.py:442
  270.3 9.8 %custom-call.17 = f32[1,128,128]{1,2,0:T(8,128)S(1)} custom-call(f32[1,128,128]{2,1,0:T(8,128)S(1)} %copy.226), custom_call_target="InvertDiagBlocksLowerTriangular" | custom-call | tf_op jit(solution)/shard_map/jit(_solve_triangular)/triangular_solve/custom-call.0 | solution.py:445
  281.4 11.7 %custom-call.18 = f32[128,128]{1,0:T(8,128)S(1)} custom-call(f32[128,128]{1,0:T(8,128)S(1)} %copy.233), custom_call_target="Cholesky" | custom-call | tf_op jit(solution)/shard_map/jit(cholesky)/cholesky/custom-call.1 | solution.py:442
  295.2 10.0 %custom-call.19 = f32[1,128,128]{1,2,0:T(8,128)S(1)} custom-call(f32[1,128,128]{2,1,0:T(8,128)S(1)} %get-tuple-element.231), custom_call_target="InvertDiagBlocksLowerTriangular" | custom-call | tf_op jit(solution)/shard_map/jit(_solve_triangular)/triangular_solve/custom-call.0 | solution.py:445
  306.0 18.8 %all-gather.10.cloned.1.call-done = f32[2048,256]{0,1:T(8,128)} async-done(((f32[512,256]{0,1:T(8,128)}), f32[2048,256]{0,1:T(8,128)}) %all-gather.10.cloned.1.call-update) | async-done | bytes 2097168 | tf_op jit(solution)/shard_map/all_gather | solution.py:518
  324.9 2.7 reshape.1159
  327.5 3.1 collective-permute-start.15
  335.3 2.8 constant_dynamic-slice_fusion.4
  342.3 2.7 collective-permute-start.18
  345.0 3.5 collective-permute-start.19
  348.5 2.7 collective-permute-start.16
  358.7 3.0 all-to-all-start.3
  361.7 5.9 %collective-permute-done.19 = f32[512,256]{1,0:T(8,128)} collective-permute-done((f32[512,256]{1,0:T(8,128)S(1)}, f32[512,256]{1,0:T(8,128)}, u32[]{:S(2)}, u32[]{:S(2)}) %collective-permute-start.19) | collective-permute-done | bytes 524320 | tf_op jit(solution)/shard_map/ppermute | solution.py:607
  368.9 2.9 pad_maximum_fusion.2.raw_ref
  371.8 8.8 %shard_map.49 = f32[832,8,128]{2,1,0:T(8,128)} custom-call(s32[32,82]{1,0:T(8,128)S(1)} %add_select_fusion.13.slot_ref, f32[32,82,8,128]{3,2,1,0:T(8,128)} %all-to-all-done.2.arrived_ref), custom_call_target="tpu_custom_call" | custom-call | tf_op jit(solution)/shard_map/pallas_call | solution.py:155
  380.6 6.9 %all-to-all-start.4 = ((f32[16,52,8,128]{3,2,1,0:T(8,128)}), f32[16,52,8,128]{3,2,1,0:T(8,128)S(1)}, u32[]{:S(2)}, u32[]{:S(2)}) async-start(f32[16,52,8,128]{3,2,1,0:T(8,128)} %bitcast.47), calls=%async_computation.6 | async-start | bytes 6815744 | tf_op jit(solution)/shard_map/all_to_all | solution.py:644
  393.0 5.6 %copy.240.raw_ref = f32[4096,256]{1,0:T(8,128)} copy(f32[4096,256]{0,1:T(8,128)} %all-gather.8.cloned.1.call-done) | data formatting | bytes 8388608 | tf_op jit(solution)/shard_map/optimization_barrier | solution.py:517
  409.1 5.1 %shard_map.50 = (f32[4096,256]{1,0:T(8,128)S(1)}, bf16[4096,768]{1,0:T(8,128)(2,1)S(1)}) custom-call(f32[4096,256]{1,0:T(8,128)S(1)} %copy-done.7, f32[256,256]{1,0:T(8,128)S(1)} %copy-done.14), custom_call_target="tpu_custom_call" | custom-call | tf_op jit(solution)/shard_map/pallas_call | solution.py:309
  418.8 3.6 shard_map.51
  425.4 50.4 %shard_map.52.partial_ref = f32[4096,2048]{1,0:T(8,128)} custom-call(s32[32,82]{1,0:T(8,128)} %get-tuple-element.265.code_ref, s32[32,82]{1,0:T(8,128)} %iota_subtract_fusion.run_ref, s32[2]{0:T(128)S(1)} %copy-done.31, f32[4096,2048]{1,0:T(8,128)} %front_ref.3, f32[4096,256]{1,0:T(8,128)} %copy-done.12, bf16[4096,768]{1,0:T(8,128)(2,1)} %copy-done.11, ...), custom_call_target="tpu_custom_call" | custom-call | tf_op jit(solution)/shard_map/pallas_call | solution.py:425
  478.0 13.8 %shard_map.53 = f32[4096,2048]{1,0:T(8,128)} custom-call(s32[832]{0:T(1024)S(1)} %get-tuple-element.188.block_ref, s32[832]{0:T(1024)S(1)} %get-tuple-element.187.unit_ref, s32[832]{0:T(1024)S(1)} %get-tuple-element.186.index_ref, s32[1]{0:T(128)} %bitcast.44.count_ref, f32[4096,2048]{1,0:T(8,128)} %shard_map.52.partial_ref, ...), custom_call_target="tpu_custom_call", output_to_operand_aliasing={{}: (4, {})} | custom-call | tf_op jit(solution)/shard_map/pallas_call | solution.py:234
  (181 shorter events, 66.0 us)
Async XLA Ops:
  8.0 9.6 %copy-start.30 = (s32[32,128]{1,0:T(8,128)}, s32[32,128]{1,0:T(8,128)S(1)}, u32[]{:S(2)}) copy-start(s32[32,128]{1,0:T(8,128)S(1)} %get-tuple-element.299) | copy-start | bytes 49156
  9.3 187.5 %copy-start.26 = (s32[32,128]{1,0:T(8,128)}, s32[32,128]{1,0:T(8,128)S(1)}, u32[]{:S(2)}) copy-start(s32[32,128]{1,0:T(8,128)S(1)} %convert_reduce_fusion.3) | copy-start | bytes 49156
  17.6 4.5 copy-start.27
  17.7 32.8 %collective-permute-start.12 = (f32[5,128,128]{2,1,0:T(8,128)S(1)}, f32[5,128,128]{2,1,0:T(8,128)S(1)}, u32[]{:S(2)}, u32[]{:S(2)}) collective-permute-start(f32[5,128,128]{2,1,0:T(8,128)S(1)} %get-tuple-element.254), channel_id=1, source_target_pairs={{0,24},{8,0},{16,8},{24,16},{1,25},{9,1},{17,9},{25,17},{2,26},{10... | collective-permute-start | bytes 983048 | tf_op jit(solution)/shard_map/ppermute | solution.py:502
  21.7 28.8 %collective-permute-start.11 = (f32[5,128,128]{2,1,0:T(8,128)S(1)}, f32[5,128,128]{2,1,0:T(8,128)S(1)}, u32[]{:S(2)}, u32[]{:S(2)}) collective-permute-start(f32[5,128,128]{2,1,0:T(8,128)S(1)} %get-tuple-element.255), channel_id=1, source_target_pairs={{0,16},{8,24},{16,0},{24,8},{1,17},{9,25},{17,1},{25,9},{2,18},{10... | collective-permute-start | bytes 983048 | tf_op jit(solution)/shard_map/ppermute | solution.py:502
  21.8 28.8 %collective-permute-start.10 = (f32[5,128,128]{2,1,0:T(8,128)S(1)}, f32[5,128,128]{2,1,0:T(8,128)S(1)}, u32[]{:S(2)}, u32[]{:S(2)}) collective-permute-start(f32[5,128,128]{2,1,0:T(8,128)S(1)} %get-tuple-element.256), channel_id=1, source_target_pairs={{0,8},{8,16},{16,24},{24,0},{1,9},{9,17},{17,25},{25,1},{2,10},{10... | collective-permute-start | bytes 983048 | tf_op jit(solution)/shard_map/ppermute | solution.py:502
  46.3 4.2 copy-start.9
  53.7 2.1 copy-start.8
  67.0 291.7 %all-to-all-start.2 = ((f32[32,82,8,128]{3,2,1,0:T(8,128)}), f32[32,82,8,128]{3,2,1,0:T(8,128)}, u32[]{:S(2)}, u32[]{:S(2)}) async-start(f32[32,82,8,128]{3,2,1,0:T(8,128)} %copy-done.9), calls=%async_computation.3 | async-start | bytes 21495808 | tf_op jit(solution)/shard_map/all_to_all | solution.py:566
  72.1 124.0 %reduce-scatter.3.cloned.1.call-start = ((), (), s32[]{:S(2)}) async-start(), calls=%async_computation.7 | async-start | bytes 4718592 | tf_op jit(solution)/shard_map/reduce_scatter | solution.py:515
  77.8 177.2 %all-gather.8.cloned.1.call-start = ((), (), s32[]{:S(2)}) async-start(), calls=%async_computation.8 | async-start | bytes 4718592 | tf_op jit(solution)/shard_map/all_gather | solution.py:516
  196.1 128.8 %all-gather.10.cloned.1.call-start = ((), (), s32[]{:S(2)}) async-start(), calls=%async_computation.9 | async-start | bytes 2621440 | tf_op jit(solution)/shard_map/all_gather | solution.py:518
  327.5 17.4 %collective-permute-start.15 = (f32[256,256]{0,1:T(8,128)S(1)}, f32[256,256]{0,1:T(8,128)}, u32[]{:S(2)}, u32[]{:S(2)}) collective-permute-start(f32[256,256]{0,1:T(8,128)S(1)} %fusion.34), channel_id=1, source_target_pairs={{0,24},{1,25},{2,26},{3,27},{4,28},{5,29},{6,30},{7,31}} | collective-permute-start | bytes 786440 | tf_op jit(solution)/shard_map/ppermute | solution.py:611
  330.6 17.8 %collective-permute-start.14 = (f32[256,256]{0,1:T(8,128)S(1)}, f32[256,256]{0,1:T(8,128)}, u32[]{:S(2)}, u32[]{:S(2)}) collective-permute-start(f32[256,256]{0,1:T(8,128)S(1)} %fusion.34), channel_id=1, source_target_pairs={{0,16},{1,17},{2,18},{3,19},{4,20},{5,21},{6,22},{7,23}} | collective-permute-start | bytes 786440 | tf_op jit(solution)/shard_map/ppermute | solution.py:611
  333.3 23.5 %collective-permute-start.13 = (f32[256,256]{0,1:T(8,128)S(1)}, f32[256,256]{0,1:T(8,128)}, u32[]{:S(2)}, u32[]{:S(2)}) collective-permute-start(f32[256,256]{0,1:T(8,128)S(1)} %fusion.34), channel_id=1, source_target_pairs={{0,8},{1,9},{2,10},{3,11},{4,12},{5,13},{6,14},{7,15}} | collective-permute-start | bytes 786440 | tf_op jit(solution)/shard_map/ppermute | solution.py:611
  338.1 13.1 %copy-start.25 = (s32[32,82]{1,0:T(8,128)S(1)}, s32[32,82]{1,0:T(8,128)}, u32[]{:S(2)}) copy-start(s32[32,82]{1,0:T(8,128)} %reduce_sum.174) | copy-start | bytes 31492
  341.6 20.1 %collective-permute-start.17 = (f32[512,256]{1,0:T(8,128)S(1)}, f32[512,256]{1,0:T(8,128)S(1)}, u32[]{:S(2)}, u32[]{:S(2)}) collective-permute-start(f32[512,256]{1,0:T(8,128)S(1)} %bitcast.190), channel_id=1, source_target_pairs={{0,2},{1,4},{2,6},{3,0},{4,3},{5,5},{6,7},{7,1},{8,10},{9,12},{10,... | collective-permute-start | bytes 1572872 | tf_op jit(solution)/shard_map/ppermute | solution.py:607
  342.3 19.4 %collective-permute-start.18 = (f32[512,256]{1,0:T(8,128)S(1)}, f32[512,256]{1,0:T(8,128)}, u32[]{:S(2)}, u32[]{:S(2)}) collective-permute-start(f32[512,256]{1,0:T(8,128)S(1)} %bitcast.189), channel_id=1, source_target_pairs={{0,4},{1,6},{2,0},{3,2},{4,5},{5,7},{6,1},{7,3},{8,12},{9,14},{10,... | collective-permute-start | bytes 1572872 | tf_op jit(solution)/shard_map/ppermute | solution.py:607
  345.0 22.7 %collective-permute-start.19 = (f32[512,256]{1,0:T(8,128)S(1)}, f32[512,256]{1,0:T(8,128)}, u32[]{:S(2)}, u32[]{:S(2)}) collective-permute-start(f32[512,256]{1,0:T(8,128)S(1)} %bitcast.188), channel_id=1, source_target_pairs={{0,6},{1,0},{2,2},{3,4},{4,7},{5,1},{6,3},{7,5},{8,14},{9,8},{10,1... | collective-permute-start | bytes 1572872 | tf_op jit(solution)/shard_map/ppermute | solution.py:607
  348.5 20.5 %collective-permute-start.16 = (f32[512,256]{1,0:T(8,128)S(1)}, f32[512,256]{1,0:T(8,128)}, u32[]{:S(2)}, u32[]{:S(2)}) collective-permute-start(f32[512,256]{1,0:T(8,128)S(1)} %bitcast.187), channel_id=1, source_target_pairs={{0,0},{1,2},{2,4},{3,6},{4,1},{5,3},{6,5},{7,7},{8,8},{9,10},{10,1... | collective-permute-start | bytes 1572872 | tf_op jit(solution)/shard_map/ppermute | solution.py:607
  358.7 21.9 %all-to-all-start.3 = ((s32[32,1,53]{2,1,0:T(1,128)}), s32[32,1,53]{2,1,0:T(1,128)S(1)}, u32[]{:S(2)}, u32[]{:S(2)}) async-start(s32[32,1,53]{2,1,0:T(1,128)} %bitcast.33), calls=%async_computation.5 | async-start | bytes 32768 | tf_op jit(solution)/shard_map/all_to_all | solution.py:620
  380.6 7.5 %copy-start.33 = (pred[32,82]{1,0:T(8,128)(4,1)S(1)}, pred[32,82]{1,0:T(8,128)(4,1)}, u32[]{:S(2)}) copy-start(pred[32,82]{1,0:T(8,128)(4,1)} %get-tuple-element.225) | copy-start | bytes 7876
  380.6 97.4 %all-to-all-start.4 = ((f32[16,52,8,128]{3,2,1,0:T(8,128)}), f32[16,52,8,128]{3,2,1,0:T(8,128)S(1)}, u32[]{:S(2)}, u32[]{:S(2)}) async-start(f32[16,52,8,128]{3,2,1,0:T(8,128)} %bitcast.47), calls=%async_computation.6 | async-start | bytes 6815744 | tf_op jit(solution)/shard_map/all_to_all | solution.py:644
  406.0 2.2 copy-start.7
  408.2 0.9 copy-start.14
  409.1 9.6 %copy-start.10 = (f32[4,512,256]{2,1,0:T(8,128)S(1)}, f32[4,512,256]{2,1,0:T(8,128)}, u32[]{:S(2)}) copy-start(f32[4,512,256]{2,1,0:T(8,128)} %pad_maximum_fusion.2.raw_ref) | copy-start | bytes 6291460
  414.2 2.6 copy-start.11
  416.8 1.9 copy-start.12
  418.8 6.7 %copy-start.31 = (s32[2]{0:T(128)S(1)}, s32[2]{0:T(128)}, u32[]{:S(2)}) copy-start(s32[2]{0:T(128)} %pad_add_fusion.2.place_ref) | copy-start | bytes 28
  422.3 1.7 copy-start.13
  424.1 1.4 copy-start.15
  478.0 13.8 %copy-start.28 = (s32[128]{0:T(128)S(1)}, s32[128]{0:T(128)}, u32[]{:S(2)}) copy-start(s32[128]{0:T(128)} %valid_ref.1) | copy-start | bytes 1540
Sparse Core Ops, SparseCore 0:
  77.9 118.1 reduce-scatter.2
  198.1 56.7 all-gather.7
  256.6 68.2 all-gather.9
where the time goes:
time: 508 us; the launch traced here: 500 us
  waiting for transfers between devices  190 us (37%)
  Pallas kernels  113 us (22%)
  other arithmetic  80.2 us (16%)
  local copies, waits for them, and re-layouts  49.8 us (10%)
  starting transfers between devices  36.1 us (7%)
  between operations  17 us (3%)
  blocking collectives  11.3 us (2%)
    reduce_scatter x1, waiting for transfers between devices, gather_panel(): chunk = lax.psum_scatter(partial, 'col', scatter_dimension=0, tiled=True)  118 us
    pallas_call x1, Pallas kernels, finish(): pl.pallas_call(functools.partial(final_kernel, cols_blocks, runs), grid=(...  50.4 us
    all_gather x1, waiting for transfers between devices, gather_panel(): raw_rows = lax.all_gather(chunk, 'col', axis=0, tiled=True)  45.7 us
    another operation x6, other arithmetic, lower_of(): return jnp.linalg.cholesky(jnp.tril(block) + jnp.tril(block, -1).T)  25 us
    another operation x5, other arithmetic, inverse_of(): jax.scipy.linalg.solve_triangular(block, jnp.eye(NB, dtype=jnp.float32),...  22.5 us
    pallas_call x1, Pallas kernels, spread(): pl.pallas_call(functools.partial(spread_kernel, width, stride), out_shape...  21.1 us
    all_gather x1, waiting for transfers between devices, gather_panel(): return (lax.all_gather(chunk, 'row', axis=0), raw_rows)  18.8 us
    unnamed x33, local copies, waits for them, and re-layouts  18 us
  transfers between devices with their start and end apart: 16, of which 5 were waited for; matrix products, arithmetic and copies ran while one was open for 22% of the time, Pallas kernels for 18%

commit v1 on v0

--- a/solution.py
+++ b/solution.py
@@ -514,7 +514,7 @@
     def gather_panel(partial):
         chunk = lax.psum_scatter(partial, "col", scatter_dimension=0, tiled=True)
         raw_rows = lax.all_gather(chunk, "col", axis=0, tiled=True)
-        chunk, raw_rows = lax.optimization_barrier((chunk, raw_rows))
+        chunk, _ = lax.optimization_barrier((chunk, raw_rows[:8, :NB]))
         return lax.all_gather(chunk, "row", axis=0), raw_rows
 
     panel_depth = (capacity * 5 + 7) // 8
@@ -590,8 +590,9 @@
         notes, relay_codes.reshape(1, half_count, pass_on).astype(jnp.int32), (device_now // half_count, 0, 0)
     )
     notes = notes.at[:, :, pass_on].set(failed.astype(jnp.int32))
-    def chain(gathered, raw_rows):
+    def chain(gathered, raw_rows, tables):
         diagonal = jnp.where(row_now == 0, raw_rows[:TOTAL], jnp.eye(TOTAL, dtype=jnp.float32))
+        diagonal, tables = lax.optimization_barrier((diagonal, tables))
         lower, inverse = factor(diagonal)
         known = jnp.where(row_now == 0, inverse, 0.0)
         gathered, known = lax.optimization_barrier((gathered, known))
@@ -609,19 +610,21 @@
         inverse = known
         for other in range(1, row_count):
             inverse += lax.ppermute(known, "row", [(0, other)])
-        return known, inverse, jnp.stack(chunks), order.astype(jnp.int32), lower
+        return known, inverse, chunks, order.astype(jnp.int32), lower, tables
 
     def solve(raw_rows, inverse, chunks, order):
         rows = solve_rows(raw_rows, inverse)
-        return rows, solve_cols(chunks, order, inverse)
-
-    known, inverse, chunks, order, lower = chain(gathered, raw_rows)
+        return rows, solve_cols(jnp.stack(chunks), order, inverse)
+
+    relay_slot = relay_slot.reshape(device_count, width)
+    tables = (notes, relay_slot, direct_codes, direct_runs)
+    known, inverse, chunks, order, lower, tables = chain(gathered, raw_rows, tables)
+    notes, relay_slot, direct_codes, direct_runs = tables
     notes, arrived, known = lax.optimization_barrier((notes, arrived, known))
     notes = lax.all_to_all(
         notes.reshape(device_count, pass_on + 1), ("row", "col"), 0, 0, tiled=True
     )
     relay_codes = lax.dynamic_slice_in_dim(notes, half_base, half_count, 0)[:, :pass_on]
-    relay_slot = relay_slot.reshape(device_count, width)
 
     flat = relay_codes.reshape(-1)
     unit_row, relay_col = flat // cols_blocks, flat % cols_blocks
@@ -662,7 +665,7 @@
         arrived = lax.all_to_all(
             packed.reshape(device_count, capacity, side, side), ("row", "col"), 0, 0, tiled=True
         )
-        _, inverse, chunks, order, lower = chain(gathered, raw_rows)
+        _, inverse, chunks, order, lower, _ = chain(gathered, raw_rows, ())
         rows, cols = solve(raw_rows, inverse, chunks, order)
         return finish(
             front, rows, cols, lower, arrived, codes, jnp.ones_like(codes), place, cols_blocks

time: 508 us -> 567 us (1.12)
  the two profiles are of different devices: /device:TPU:5 before, /device:TPU:6 now
where the time goes in v1:
time: 567 us; the launch traced here: 556 us
  waiting for transfers between devices  255 us (45%)
  Pallas kernels  110 us (19%)
  other arithmetic  75.4 us (13%)
  local copies, waits for them, and re-layouts  46.3 us (8%)
  starting transfers between devices  38.6 us (7%)
  between operations  16.9 us (3%)
  blocking collectives  10.7 us (2%)
    reduce_scatter x1, waiting for transfers between devices, gather_panel(): chunk = lax.psum_scatter(partial, 'col', scatter_dimension=0, tiled=True)  116 us
    all_gather x1, waiting for transfers between devices, gather_panel(): return (lax.all_gather(chunk, 'row', axis=0), raw_rows)  82.5 us
    all_gather x1, waiting for transfers between devices, gather_panel(): raw_rows = lax.all_gather(chunk, 'col', axis=0, tiled=True)  54.5 us
    pallas_call x1, Pallas kernels, finish(): pl.pallas_call(functools.partial(final_kernel, cols_blocks, runs), grid=(...  50.7 us
    another operation x6, other arithmetic, lower_of(): return jnp.linalg.cholesky(jnp.tril(block) + jnp.tril(block, -1).T)  24.9 us
    another operation x5, other arithmetic, inverse_of(): jax.scipy.linalg.solve_triangular(block, jnp.eye(NB, dtype=jnp.float32),...  22.6 us
    pallas_call x1, Pallas kernels, spread(): pl.pallas_call(functools.partial(spread_kernel, width, stride), out_shape...  20.3 us
    unnamed x39, local copies, waits for them, and re-layouts  19.3 us
  transfers between devices with their start and end apart: 16, of which 5 were waited for; matrix products, arithmetic and copies ran while one was open for 17% of the time, Pallas kernels for 16%

profile of v1, /device:TPU:6, one launch (start us, length us, event | category | flops | bytes accessed | tf_op | source)
XLA Modules:
  0.0 555.9 jit_solution(5020142221840337892)
XLA Ops:
  10.6 7.2 %shard_map.46 = f32[20,128,128]{2,1,0:T(8,128)S(1)} custom-call(s32[128]{0:T(128)S(1)} %get-tuple-element.281.slot_ref, s32[128]{0:T(128)} %valid_ref.1, f32[128,128,128]{2,1,0:T(8,128)} %tiles_ref.1), custom_call_target="tpu_custom_call" | custom-call | tf_op jit(solution)/shard_map/pallas_call | solution.py:56
  18.0 3.4 collective-permute-start.12
  25.5 20.3 %shard_map.48 = (f32[32,82,8,128]{3,2,1,0:T(8,128)S(1)}, s32[32,128]{1,0:T(8,128)S(1)}) custom-call(s32[6,128]{1,0:T(8,128)S(1)} %select_reduce_fusion.7.meta_ref, s32[2,16]{1,0:T(2,128)S(1)} %select_reduce_fusion.11.empty_ref, s32[3]{0:T(128)S(1)} %pad_add_fusion.1.count_ref, f32[128,16,8,128]{3,2,1,0:T(8,128)} %bitcast.182), custom_call_target="tpu_custom_call" | custom-call | tf_op jit(solution)/shard_map/pallas_call | solution.py:122
  45.8 4.2 copy-done.9
  50.1 3.0 shard_map.47
  55.0 5.6 %copy.217 = f32[4096,256]{0,1:T(8,128)} copy(f32[4096,256]{1,0:T(8,128)} %copy-done.8) | data formatting | bytes 8388608 | tf_op jit(solution)/shard_map/optimization_barrier | solution.py:562
  60.6 10.7 %all_to_all.39 = s32[32,1,82]{2,1,0:T(1,128)S(1)} all-to-all(s32[32,1,82]{2,1,0:T(1,128)S(1)} %bitcast.181), channel_id=1, replica_groups=mesh['row'=4,'col'=8] {'row','col'}, dimensions={0} | all-to-all | bytes 20992 | tf_op jit(solution)/shard_map/all_to_all | solution.py:564
  71.3 5.6 %all-to-all-start.2 = ((f32[32,82,8,128]{3,2,1,0:T(8,128)}), f32[32,82,8,128]{3,2,1,0:T(8,128)}, u32[]{:S(2)}, u32[]{:S(2)}) async-start(f32[32,82,8,128]{3,2,1,0:T(8,128)} %copy-done.9), calls=%async_computation.4 | async-start | bytes 21495808 | tf_op jit(solution)/shard_map/all_to_all | solution.py:566
  77.0 115.6 %reduce-scatter.3.cloned.1.call-done = f32[512,256]{0,1:T(8,128)} async-done(((f32[4096,256]{0,1:T(8,128)}), f32[512,256]{0,1:T(8,128)}) %reduce-scatter.3.cloned.1.call-update) | async-done | bytes 524304 | tf_op jit(solution)/shard_map/reduce_scatter | solution.py:515
  200.0 6.1 %convert_reduce_fusion.1 = s32[2624]{0:T(1024)S(1)} fusion(s32[2624]{0:T(1024)S(1)} %get-tuple-element.280, s32[2624]{0:T(1024)S(1)} %get-tuple-element.279), kind=kLoop, calls=%fused_computation.99 | loop fusion | flops 34424256 | bytes 31488 | tf_op jit(solution)/shard_map/reduce_sum | solution.py:579
  209.8 82.5 %all-gather.10.cloned.1.call-done = f32[2048,256]{0,1:T(8,128)} async-done(((f32[512,256]{0,1:T(8,128)}), f32[2048,256]{0,1:T(8,128)}) %all-gather.10.cloned.1.call-update) | async-done | bytes 2097168 | tf_op jit(solution)/shard_map/all_gather | solution.py:518
  292.3 2.8 reshape.1159
  295.2 54.5 %all-gather.8.cloned.1.call-done = f32[4096,256]{0,1:T(8,128)} async-done(((f32[512,256]{0,1:T(8,128)}), f32[4096,256]{0,1:T(8,128)}) %all-gather.8.cloned.1.call-update) | async-done | bytes 4194320 | tf_op jit(solution)/shard_map/all_gather | solution.py:516
  351.0 11.7 %custom-call.16 = f32[128,128]{1,0:T(8,128)S(1)} custom-call(f32[128,128]{1,0:T(8,128)S(1)} %copy.224), custom_call_target="Cholesky" | custom-call | tf_op jit(solution)/shard_map/jit(cholesky)/cholesky/custom-call.1 | solution.py:442
  365.0 9.8 %custom-call.17 = f32[1,128,128]{1,2,0:T(8,128)S(1)} custom-call(f32[1,128,128]{2,1,0:T(8,128)S(1)} %copy.227), custom_call_target="InvertDiagBlocksLowerTriangular" | custom-call | tf_op jit(solution)/shard_map/jit(_solve_triangular)/triangular_solve/custom-call.0 | solution.py:445
  376.0 11.7 %custom-call.18 = f32[128,128]{1,0:T(8,128)S(1)} custom-call(f32[128,128]{1,0:T(8,128)S(1)} %copy.234), custom_call_target="Cholesky" | custom-call | tf_op jit(solution)/shard_map/jit(cholesky)/cholesky/custom-call.1 | solution.py:442
  389.8 10.2 %custom-call.19 = f32[1,128,128]{1,2,0:T(8,128)S(1)} custom-call(f32[1,128,128]{2,1,0:T(8,128)S(1)} %get-tuple-element.235), custom_call_target="InvertDiagBlocksLowerTriangular" | custom-call | tf_op jit(solution)/shard_map/jit(_solve_triangular)/triangular_solve/custom-call.0 | solution.py:445
  400.9 5.0 collective-permute-start.15
  405.9 2.0 collective-permute-start.14
  407.8 2.8 constant_dynamic-slice_fusion.1
  419.6 2.5 collective-permute-start.19
  422.1 2.0 collective-permute-start.13
  424.1 4.7 all-to-all-start.3
  431.0 9.4 %shard_map.49 = f32[832,8,128]{2,1,0:T(8,128)} custom-call(s32[32,82]{1,0:T(8,128)S(1)} %add_select_fusion.13.slot_ref, f32[32,82,8,128]{3,2,1,0:T(8,128)} %all-to-all-done.2.arrived_ref), custom_call_target="tpu_custom_call" | custom-call | tf_op jit(solution)/shard_map/pallas_call | solution.py:155
  442.5 6.8 %all-to-all-start.4 = ((f32[16,52,8,128]{3,2,1,0:T(8,128)}), f32[16,52,8,128]{3,2,1,0:T(8,128)S(1)}, u32[]{:S(2)}, u32[]{:S(2)}) async-start(f32[16,52,8,128]{3,2,1,0:T(8,128)} %bitcast.47), calls=%async_computation.6 | async-start | bytes 6815744 | tf_op jit(solution)/shard_map/all_to_all | solution.py:647
  451.7 5.6 %copy.240.raw_ref = f32[4096,256]{1,0:T(8,128)} copy(f32[4096,256]{0,1:T(8,128)} %all-gather.8.cloned.1.call-done) | data formatting | bytes 8388608 | tf_op jit(solution)/shard_map/all_gather | solution.py:516
  463.1 2.2 copy-done.7
  466.3 5.1 shard_map.50
  471.3 2.6 copy-done.10
  477.2 3.6 shard_map.51
  483.9 50.7 %shard_map.52.partial_ref = f32[4096,2048]{1,0:T(8,128)} custom-call(s32[32,82]{1,0:T(8,128)} %get-tuple-element.145.code_ref, s32[32,82]{1,0:T(8,128)} %iota_subtract_fusion.run_ref, s32[2]{0:T(128)S(1)} %pad_add_fusion.2.place_ref, f32[4096,2048]{1,0:T(8,128)} %front_ref.3, f32[4096,256]{1,0:T(8,128)} %copy-done.11, bf16[4096,768]{1,0:T(8,128)(2,1)} %copy-done.10, ...), custom_call_target="tpu_custom_call" | custom-call | tf_op jit(solution)/shard_map/pallas_call | solution.py:425
  536.8 11.2 %shard_map.53 = f32[4096,2048]{1,0:T(8,128)} custom-call(s32[832]{0:T(1024)S(1)} %get-tuple-element.196.block_ref, s32[832]{0:T(1024)S(1)} %get-tuple-element.195.unit_ref, s32[832]{0:T(1024)S(1)} %get-tuple-element.194.index_ref, s32[1]{0:T(128)} %bitcast.40.count_ref, f32[4096,2048]{1,0:T(8,128)} %shard_map.52.partial_ref, ...), custom_call_target="tpu_custom_call", output_to_operand_aliasing={{}: (4, {})} | custom-call | tf_op jit(solution)/shard_map/pallas_call | solution.py:234
  (187 shorter events, 57.9 us)
Async XLA Ops:
  6.5 186.0 %reduce-scatter.3.cloned.1.call-start = ((), (), s32[]{:S(2)}) async-start(), calls=%async_computation.7 | async-start | bytes 4718592 | tf_op jit(solution)/shard_map/reduce_scatter | solution.py:515
  8.0 9.8 %copy-start.34 = (s32[32,128]{1,0:T(8,128)}, s32[32,128]{1,0:T(8,128)S(1)}, u32[]{:S(2)}) copy-start(s32[32,128]{1,0:T(8,128)S(1)} %get-tuple-element.307) | copy-start | bytes 49156
  9.3 184.6 %copy-start.29 = (s32[32,128]{1,0:T(8,128)}, s32[32,128]{1,0:T(8,128)S(1)}, u32[]{:S(2)}) copy-start(s32[32,128]{1,0:T(8,128)S(1)} %convert_reduce_fusion.3) | copy-start | bytes 49156
  17.9 4.5 copy-start.30
  18.0 32.0 %collective-permute-start.12 = (f32[5,128,128]{2,1,0:T(8,128)S(1)}, f32[5,128,128]{2,1,0:T(8,128)S(1)}, u32[]{:S(2)}, u32[]{:S(2)}) collective-permute-start(f32[5,128,128]{2,1,0:T(8,128)S(1)} %get-tuple-element.262), channel_id=1, source_target_pairs={{0,24},{8,0},{16,8},{24,16},{1,25},{9,1},{17,9},{25,17},{2,26},{10... | collective-permute-start | bytes 983048 | tf_op jit(solution)/shard_map/ppermute | solution.py:502
  21.4 28.6 %collective-permute-start.11 = (f32[5,128,128]{2,1,0:T(8,128)S(1)}, f32[5,128,128]{2,1,0:T(8,128)S(1)}, u32[]{:S(2)}, u32[]{:S(2)}) collective-permute-start(f32[5,128,128]{2,1,0:T(8,128)S(1)} %get-tuple-element.263), channel_id=1, source_target_pairs={{0,16},{8,24},{16,0},{24,8},{1,17},{9,25},{17,1},{25,9},{2,18},{10... | collective-permute-start | bytes 983048 | tf_op jit(solution)/shard_map/ppermute | solution.py:502
  21.4 28.6 %collective-permute-start.10 = (f32[5,128,128]{2,1,0:T(8,128)S(1)}, f32[5,128,128]{2,1,0:T(8,128)S(1)}, u32[]{:S(2)}, u32[]{:S(2)}) collective-permute-start(f32[5,128,128]{2,1,0:T(8,128)S(1)} %get-tuple-element.264), channel_id=1, source_target_pairs={{0,8},{8,16},{16,24},{24,0},{1,9},{9,17},{17,25},{25,1},{2,10},{10... | collective-permute-start | bytes 983048 | tf_op jit(solution)/shard_map/ppermute | solution.py:502
  45.8 4.2 copy-start.9
  53.0 1.9 copy-start.8
  71.3 352.9 %all-to-all-start.2 = ((f32[32,82,8,128]{3,2,1,0:T(8,128)}), f32[32,82,8,128]{3,2,1,0:T(8,128)}, u32[]{:S(2)}, u32[]{:S(2)}) async-start(f32[32,82,8,128]{3,2,1,0:T(8,128)} %copy-done.9), calls=%async_computation.4 | async-start | bytes 21495808 | tf_op jit(solution)/shard_map/all_to_all | solution.py:566
  76.9 215.4 %all-gather.10.cloned.1.call-start = ((), (), s32[]{:S(2)}) async-start(), calls=%async_computation.9 | async-start | bytes 2621440 | tf_op jit(solution)/shard_map/all_gather | solution.py:518
  192.6 157.1 %all-gather.8.cloned.1.call-start = ((), (), s32[]{:S(2)}) async-start(), calls=%async_computation.8 | async-start | bytes 4718592 | tf_op jit(solution)/shard_map/all_gather | solution.py:516
  400.9 18.7 %collective-permute-start.15 = (f32[256,256]{0,1:T(8,128)S(1)}, f32[256,256]{0,1:T(8,128)}, u32[]{:S(2)}, u32[]{:S(2)}) collective-permute-start(f32[256,256]{0,1:T(8,128)S(1)} %fusion.34), channel_id=1, source_target_pairs={{0,24},{1,25},{2,26},{3,27},{4,28},{5,29},{6,30},{7,31}} | collective-permute-start | bytes 786440 | tf_op jit(solution)/shard_map/ppermute | solution.py:612
  405.9 16.2 %collective-permute-start.14 = (f32[256,256]{0,1:T(8,128)S(1)}, f32[256,256]{0,1:T(8,128)}, u32[]{:S(2)}, u32[]{:S(2)}) collective-permute-start(f32[256,256]{0,1:T(8,128)S(1)} %fusion.34), channel_id=1, source_target_pairs={{0,16},{1,17},{2,18},{3,19},{4,20},{5,21},{6,22},{7,23}} | collective-permute-start | bytes 786440 | tf_op jit(solution)/shard_map/ppermute | solution.py:612
  414.1 26.3 %collective-permute-start.16 = (f32[512,256]{1,0:T(8,128)S(1)}, f32[512,256]{1,0:T(8,128)S(1)}, u32[]{:S(2)}, u32[]{:S(2)}) collective-permute-start(f32[512,256]{1,0:T(8,128)S(1)} %bitcast.190), channel_id=1, source_target_pairs={{0,0},{1,2},{2,4},{3,6},{4,1},{5,3},{6,5},{7,7},{8,8},{9,10},{10,1... | collective-permute-start | bytes 1572872 | tf_op jit(solution)/shard_map/ppermute | solution.py:608
  416.1 25.6 %collective-permute-start.17 = (f32[512,256]{1,0:T(8,128)S(1)}, f32[512,256]{1,0:T(8,128)S(1)}, u32[]{:S(2)}, u32[]{:S(2)}) collective-permute-start(f32[512,256]{1,0:T(8,128)S(1)} %bitcast.189), channel_id=1, source_target_pairs={{0,2},{1,4},{2,6},{3,0},{4,3},{5,5},{6,7},{7,1},{8,10},{9,12},{10,... | collective-permute-start | bytes 1572872 | tf_op jit(solution)/shard_map/ppermute | solution.py:608
  418.0 23.7 %collective-permute-start.18 = (f32[512,256]{1,0:T(8,128)S(1)}, f32[512,256]{1,0:T(8,128)}, u32[]{:S(2)}, u32[]{:S(2)}) collective-permute-start(f32[512,256]{1,0:T(8,128)S(1)} %bitcast.188), channel_id=1, source_target_pairs={{0,4},{1,6},{2,0},{3,2},{4,5},{5,7},{6,1},{7,3},{8,12},{9,14},{10,... | collective-permute-start | bytes 1572872 | tf_op jit(solution)/shard_map/ppermute | solution.py:608
  419.6 22.1 %collective-permute-start.19 = (f32[512,256]{1,0:T(8,128)S(1)}, f32[512,256]{1,0:T(8,128)}, u32[]{:S(2)}, u32[]{:S(2)}) collective-permute-start(f32[512,256]{1,0:T(8,128)S(1)} %bitcast.187), channel_id=1, source_target_pairs={{0,6},{1,0},{2,2},{3,4},{4,7},{5,1},{6,3},{7,5},{8,14},{9,8},{10,1... | collective-permute-start | bytes 1572872 | tf_op jit(solution)/shard_map/ppermute | solution.py:608
  422.1 7.0 %collective-permute-start.13 = (f32[256,256]{0,1:T(8,128)S(1)}, f32[256,256]{0,1:T(8,128)}, u32[]{:S(2)}, u32[]{:S(2)}) collective-permute-start(f32[256,256]{0,1:T(8,128)S(1)} %fusion.34), channel_id=1, source_target_pairs={{0,8},{1,9},{2,10},{3,11},{4,12},{5,13},{6,14},{7,15}} | collective-permute-start | bytes 786440 | tf_op jit(solution)/shard_map/ppermute | solution.py:612
  424.1 17.6 %all-to-all-start.3 = ((s32[32,1,53]{2,1,0:T(1,128)}), s32[32,1,53]{2,1,0:T(1,128)S(1)}, u32[]{:S(2)}, u32[]{:S(2)}) async-start(s32[32,1,53]{2,1,0:T(1,128)} %bitcast.203), calls=%async_computation.5 | async-start | bytes 32768 | tf_op jit(solution)/shard_map/all_to_all | solution.py:624
  440.4 1.3 copy-start.22
  442.5 94.3 %all-to-all-start.4 = ((f32[16,52,8,128]{3,2,1,0:T(8,128)}), f32[16,52,8,128]{3,2,1,0:T(8,128)S(1)}, u32[]{:S(2)}, u32[]{:S(2)}) async-start(f32[16,52,8,128]{3,2,1,0:T(8,128)} %bitcast.47), calls=%async_computation.6 | async-start | bytes 6815744 | tf_op jit(solution)/shard_map/all_to_all | solution.py:647
  449.4 34.5 %copy-start.35 = (s32[2]{0:T(128)}, s32[2]{0:T(128)S(1)}, u32[]{:S(2)}) copy-start(s32[2]{0:T(128)S(1)} %pad_add_fusion.2.place_ref) | copy-start | bytes 28
  451.7 5.6 %copy-start.28 = (f32[128,128]{1,0:T(8,128)S(1)}, f32[128,128]{1,0:T(8,128)}, u32[]{:S(2)}) copy-start(f32[128,128]{1,0:T(8,128)} %get-tuple-element.236) | copy-start | bytes 196612
  463.1 2.2 copy-start.7
  466.3 9.6 %copy-start.23 = (f32[512,256]{1,0:T(8,128)S(1)}, f32[512,256]{1,0:T(8,128)}, u32[]{:S(2)}) copy-start(f32[512,256]{1,0:T(8,128)} %copy-done.22) | copy-start | bytes 1572868
  466.3 9.6 %copy-start.25 = (f32[512,256]{1,0:T(8,128)S(1)}, f32[512,256]{1,0:T(8,128)}, u32[]{:S(2)}) copy-start(f32[512,256]{1,0:T(8,128)} %copy-done.24) | copy-start | bytes 1572868
  471.3 2.6 copy-start.10
  473.9 1.9 copy-start.11
  480.8 1.7 copy-start.12
  482.5 1.4 copy-start.14
  536.8 11.2 %copy-start.31 = (s32[128]{0:T(128)S(1)}, s32[128]{0:T(128)}, u32[]{:S(2)}) copy-start(s32[128]{0:T(128)} %valid_ref.1) | copy-start | bytes 1540
  (3 other events, 2.5 us)
Sparse Core Ops, SparseCore 0:
  60.7 131.8 reduce-scatter.2
  194.2 98.0 all-gather.9
  294.4 55.2 all-gather.7

commit v2 on v1

--- a/solution.py
+++ b/solution.py
@@ -514,7 +514,7 @@
     def gather_panel(partial):
         chunk = lax.psum_scatter(partial, "col", scatter_dimension=0, tiled=True)
         raw_rows = lax.all_gather(chunk, "col", axis=0, tiled=True)
-        chunk, _ = lax.optimization_barrier((chunk, raw_rows[:8, :NB]))
+        chunk, raw_rows = lax.optimization_barrier((chunk, raw_rows))
         return lax.all_gather(chunk, "row", axis=0), raw_rows
 
     panel_depth = (capacity * 5 + 7) // 8

time: 567 us -> 485 us (0.86)
  the two profiles are of different devices: /device:TPU:6 before, /device:TPU:23 now
where the time goes in v2:
time: 485 us; the launch traced here: 480 us
  waiting for transfers between devices  176 us (36%)
  Pallas kernels  112 us (23%)
  other arithmetic  75.2 us (16%)
  local copies, waits for them, and re-layouts  46.1 us (10%)
  starting transfers between devices  44.1 us (9%)
  between operations  16.8 us (3%)
  blocking collectives  9.18 us (2%)
    reduce_scatter x1, waiting for transfers between devices, gather_panel(): chunk = lax.psum_scatter(partial, 'col', scatter_dimension=0, tiled=True)  108 us
    all_gather x1, waiting for transfers between devices, gather_panel(): raw_rows = lax.all_gather(chunk, 'col', axis=0, tiled=True)  55.2 us
    pallas_call x1, Pallas kernels, finish(): pl.pallas_call(functools.partial(final_kernel, cols_blocks, runs), grid=(...  51.2 us
    another operation x6, other arithmetic, lower_of(): return jnp.linalg.cholesky(jnp.tril(block) + jnp.tril(block, -1).T)  24.8 us
    another operation x5, other arithmetic, inverse_of(): jax.scipy.linalg.solve_triangular(block, jnp.eye(NB, dtype=jnp.float32),...  22.6 us
    pallas_call x1, Pallas kernels, spread(): pl.pallas_call(functools.partial(spread_kernel, width, stride), out_shape...  21.5 us
    unnamed x37, local copies, waits for them, and re-layouts  18.9 us
    all_gather x1, waiting for transfers between devices, gather_panel(): return (lax.all_gather(chunk, 'row', axis=0), raw_rows)  12.8 us
  transfers between devices with their start and end apart: 16, of which 3 were waited for; matrix products, arithmetic and copies ran while one was open for 21% of the time, Pallas kernels for 19%

profile of v2, /device:TPU:23, one launch (start us, length us, event | category | flops | bytes accessed | tf_op | source)
XLA Modules:
  0.0 480.3 jit_solution(8800961030315719465)
XLA Ops:
  10.6 7.0 %shard_map.46 = f32[20,128,128]{2,1,0:T(8,128)S(1)} custom-call(s32[128]{0:T(128)S(1)} %get-tuple-element.289.slot_ref, s32[128]{0:T(128)} %valid_ref.1, f32[128,128,128]{2,1,0:T(8,128)} %tiles_ref.1), custom_call_target="tpu_custom_call" | custom-call | tf_op jit(solution)/shard_map/pallas_call | solution.py:56
  18.0 3.2 collective-permute-start.11
  24.3 21.5 %shard_map.48 = (f32[32,82,8,128]{3,2,1,0:T(8,128)S(1)}, s32[32,128]{1,0:T(8,128)S(1)}) custom-call(s32[6,128]{1,0:T(8,128)S(1)} %select_reduce_fusion.7.meta_ref, s32[2,16]{1,0:T(2,128)S(1)} %select_reduce_fusion.11.empty_ref, s32[3]{0:T(128)S(1)} %pad_add_fusion.1.count_ref, f32[128,16,8,128]{3,2,1,0:T(8,128)} %bitcast.182), custom_call_target="tpu_custom_call" | custom-call | tf_op jit(solution)/shard_map/pallas_call | solution.py:122
  45.8 4.2 copy-done.9
  50.1 3.0 shard_map.47
  53.1 2.0 copy-done.8
  55.1 9.2 %all_to_all.39 = s32[32,1,82]{2,1,0:T(1,128)S(1)} all-to-all(s32[32,1,82]{2,1,0:T(1,128)S(1)} %bitcast.181), channel_id=1, replica_groups=mesh['row'=4,'col'=8] {'row','col'}, dimensions={0} | all-to-all | bytes 20992 | tf_op jit(solution)/shard_map/all_to_all | solution.py:564
  64.3 7.9 %all-to-all-start.2 = ((f32[32,82,8,128]{3,2,1,0:T(8,128)}), f32[32,82,8,128]{3,2,1,0:T(8,128)}, u32[]{:S(2)}, u32[]{:S(2)}) async-start(f32[32,82,8,128]{3,2,1,0:T(8,128)} %copy-done.9), calls=%async_computation.4 | async-start | bytes 21495808 | tf_op jit(solution)/shard_map/all_to_all | solution.py:566
  72.3 5.6 %copy.217 = f32[4096,256]{0,1:T(8,128)} copy(f32[4096,256]{1,0:T(8,128)} %copy-done.8) | data formatting | bytes 8388608 | tf_op jit(solution)/shard_map/optimization_barrier | solution.py:562
  78.0 107.6 %reduce-scatter.3.cloned.1.call-done = f32[512,256]{0,1:T(8,128)} async-done(((f32[4096,256]{0,1:T(8,128)}), f32[512,256]{0,1:T(8,128)}) %reduce-scatter.3.cloned.1.call-update) | async-done | bytes 524304 | tf_op jit(solution)/shard_map/reduce_scatter | solution.py:515
  192.3 6.1 %convert_reduce_fusion.1 = s32[2624]{0:T(1024)S(1)} fusion(s32[2624]{0:T(1024)S(1)} %get-tuple-element.288, s32[2624]{0:T(1024)S(1)} %get-tuple-element.287), kind=kLoop, calls=%fused_computation.99 | loop fusion | flops 34424256 | bytes 31488 | tf_op jit(solution)/shard_map/reduce_sum | solution.py:579
  202.4 55.2 %all-gather.8.cloned.1.call-done = f32[4096,256]{0,1:T(8,128)} async-done(((f32[512,256]{0,1:T(8,128)}), f32[4096,256]{0,1:T(8,128)}) %all-gather.8.cloned.1.call-update) | async-done | bytes 4194320 | tf_op jit(solution)/shard_map/all_gather | solution.py:516
  258.9 11.7 %custom-call.16 = f32[128,128]{1,0:T(8,128)S(1)} custom-call(f32[128,128]{1,0:T(8,128)S(1)} %copy.224), custom_call_target="Cholesky" | custom-call | tf_op jit(solution)/shard_map/jit(cholesky)/cholesky/custom-call.1 | solution.py:442
  272.7 9.8 %custom-call.17 = f32[1,128,128]{1,2,0:T(8,128)S(1)} custom-call(f32[1,128,128]{2,1,0:T(8,128)S(1)} %copy.227), custom_call_target="InvertDiagBlocksLowerTriangular" | custom-call | tf_op jit(solution)/shard_map/jit(_solve_triangular)/triangular_solve/custom-call.0 | solution.py:445
  283.7 11.7 %custom-call.18 = f32[128,128]{1,0:T(8,128)S(1)} custom-call(f32[128,128]{1,0:T(8,128)S(1)} %copy.234), custom_call_target="Cholesky" | custom-call | tf_op jit(solution)/shard_map/jit(cholesky)/cholesky/custom-call.1 | solution.py:442
  297.5 10.3 %custom-call.19 = f32[1,128,128]{1,2,0:T(8,128)S(1)} custom-call(f32[1,128,128]{2,1,0:T(8,128)S(1)} %get-tuple-element.243), custom_call_target="InvertDiagBlocksLowerTriangular" | custom-call | tf_op jit(solution)/shard_map/jit(_solve_triangular)/triangular_solve/custom-call.0 | solution.py:445
  308.7 12.8 %all-gather.10.cloned.1.call-done = f32[2048,256]{0,1:T(8,128)} async-done(((f32[512,256]{0,1:T(8,128)}), f32[2048,256]{0,1:T(8,128)}) %all-gather.10.cloned.1.call-update) | async-done | bytes 2097168 | tf_op jit(solution)/shard_map/all_gather | solution.py:518
  321.4 2.7 reshape.1159
  326.8 2.8 constant_dynamic-slice_fusion.1
  333.8 5.0 %collective-permute-start.17 = (f32[512,256]{1,0:T(8,128)S(1)}, f32[512,256]{1,0:T(8,128)S(1)}, u32[]{:S(2)}, u32[]{:S(2)}) collective-permute-start(f32[512,256]{1,0:T(8,128)S(1)} %bitcast.189), channel_id=1, source_target_pairs={{0,2},{1,4},{2,6},{3,0},{4,3},{5,5},{6,7},{7,1},{8,10},{9,12},{10,... | collective-permute-start | bytes 1572872 | tf_op jit(solution)/shard_map/ppermute | solution.py:608
  338.9 3.3 collective-permute-start.19
  343.7 11.9 %all-to-all-start.3 = ((s32[32,1,53]{2,1,0:T(1,128)}), s32[32,1,53]{2,1,0:T(1,128)S(1)}, u32[]{:S(2)}, u32[]{:S(2)}) async-start(s32[32,1,53]{2,1,0:T(1,128)} %bitcast.203), calls=%async_computation.5 | async-start | bytes 32768 | tf_op jit(solution)/shard_map/all_to_all | solution.py:624
  357.5 8.8 %shard_map.49 = f32[832,8,128]{2,1,0:T(8,128)} custom-call(s32[32,82]{1,0:T(8,128)S(1)} %add_select_fusion.13.slot_ref, f32[32,82,8,128]{3,2,1,0:T(8,128)} %all-to-all-done.2.arrived_ref), custom_call_target="tpu_custom_call" | custom-call | tf_op jit(solution)/shard_map/pallas_call | solution.py:155
  367.3 7.6 %all-to-all-start.4 = ((f32[16,52,8,128]{3,2,1,0:T(8,128)}), f32[16,52,8,128]{3,2,1,0:T(8,128)S(1)}, u32[]{:S(2)}, u32[]{:S(2)}) async-start(f32[16,52,8,128]{3,2,1,0:T(8,128)} %bitcast.47), calls=%async_computation.6 | async-start | bytes 6815744 | tf_op jit(solution)/shard_map/all_to_all | solution.py:647
  374.9 5.6 %copy.240.raw_ref = f32[4096,256]{1,0:T(8,128)} copy(f32[4096,256]{0,1:T(8,128)} %all-gather.8.cloned.1.call-done) | data formatting | bytes 8388608 | tf_op jit(solution)/shard_map/optimization_barrier | solution.py:517
  387.9 2.2 copy-done.7
  391.1 5.1 %shard_map.50 = (f32[4096,256]{1,0:T(8,128)S(1)}, bf16[4096,768]{1,0:T(8,128)(2,1)S(1)}) custom-call(f32[4096,256]{1,0:T(8,128)S(1)} %copy-done.7, f32[256,256]{1,0:T(8,128)S(1)} %copy-done.13), custom_call_target="tpu_custom_call" | custom-call | tf_op jit(solution)/shard_map/pallas_call | solution.py:309
  396.2 2.6 copy-done.10
  398.8 1.9 copy-done.11
  402.0 3.6 shard_map.51
  408.7 51.2 %shard_map.52.partial_ref = f32[4096,2048]{1,0:T(8,128)} custom-call(s32[32,82]{1,0:T(8,128)} %get-tuple-element.151.code_ref, s32[32,82]{1,0:T(8,128)} %iota_subtract_fusion.run_ref, s32[2]{0:T(128)S(1)} %pad_add_fusion.2.place_ref, f32[4096,2048]{1,0:T(8,128)} %front_ref.3, f32[4096,256]{1,0:T(8,128)} %copy-done.11, bf16[4096,768]{1,0:T(8,128)(2,1)} %copy-done.10, ...), custom_call_target="tpu_custom_call" | custom-call | tf_op jit(solution)/shard_map/pallas_call | solution.py:425
  462.1 11.6 %shard_map.53 = f32[4096,2048]{1,0:T(8,128)} custom-call(s32[832]{0:T(1024)S(1)} %get-tuple-element.204.block_ref, s32[832]{0:T(1024)S(1)} %get-tuple-element.203.unit_ref, s32[832]{0:T(1024)S(1)} %get-tuple-element.202.index_ref, s32[1]{0:T(128)} %bitcast.40.count_ref, f32[4096,2048]{1,0:T(8,128)} %shard_map.52.partial_ref, ...), custom_call_target="tpu_custom_call", output_to_operand_aliasing={{}: (4, {})} | custom-call | tf_op jit(solution)/shard_map/pallas_call | solution.py:234
  (185 shorter events, 49.1 us)
Async XLA Ops:
  8.0 9.6 %copy-start.33 = (s32[32,128]{1,0:T(8,128)}, s32[32,128]{1,0:T(8,128)S(1)}, u32[]{:S(2)}) copy-start(s32[32,128]{1,0:T(8,128)S(1)} %get-tuple-element.315) | copy-start | bytes 49156
  9.3 176.9 %copy-start.28 = (s32[32,128]{1,0:T(8,128)}, s32[32,128]{1,0:T(8,128)S(1)}, u32[]{:S(2)}) copy-start(s32[32,128]{1,0:T(8,128)S(1)} %convert_reduce_fusion.3) | copy-start | bytes 49156
  17.6 3.6 copy-start.29
  17.7 32.2 %collective-permute-start.12 = (f32[5,128,128]{2,1,0:T(8,128)S(1)}, f32[5,128,128]{2,1,0:T(8,128)S(1)}, u32[]{:S(2)}, u32[]{:S(2)}) collective-permute-start(f32[5,128,128]{2,1,0:T(8,128)S(1)} %get-tuple-element.270), channel_id=1, source_target_pairs={{0,24},{8,0},{16,8},{24,16},{1,25},{9,1},{17,9},{25,17},{2,26},{10... | collective-permute-start | bytes 983048 | tf_op jit(solution)/shard_map/ppermute | solution.py:502
  18.0 32.0 %collective-permute-start.11 = (f32[5,128,128]{2,1,0:T(8,128)S(1)}, f32[5,128,128]{2,1,0:T(8,128)S(1)}, u32[]{:S(2)}, u32[]{:S(2)}) collective-permute-start(f32[5,128,128]{2,1,0:T(8,128)S(1)} %get-tuple-element.271), channel_id=1, source_target_pairs={{0,16},{8,24},{16,0},{24,8},{1,17},{9,25},{17,1},{25,9},{2,18},{10... | collective-permute-start | bytes 983048 | tf_op jit(solution)/shard_map/ppermute | solution.py:502
  21.2 28.8 %collective-permute-start.10 = (f32[5,128,128]{2,1,0:T(8,128)S(1)}, f32[5,128,128]{2,1,0:T(8,128)S(1)}, u32[]{:S(2)}, u32[]{:S(2)}) collective-permute-start(f32[5,128,128]{2,1,0:T(8,128)S(1)} %get-tuple-element.272), channel_id=1, source_target_pairs={{0,8},{8,16},{16,24},{24,0},{1,9},{9,17},{17,25},{25,1},{2,10},{10... | collective-permute-start | bytes 983048 | tf_op jit(solution)/shard_map/ppermute | solution.py:502
  45.8 4.2 copy-start.9
  53.1 2.1 copy-start.8
  64.3 279.3 %all-to-all-start.2 = ((f32[32,82,8,128]{3,2,1,0:T(8,128)}), f32[32,82,8,128]{3,2,1,0:T(8,128)}, u32[]{:S(2)}, u32[]{:S(2)}) async-start(f32[32,82,8,128]{3,2,1,0:T(8,128)} %copy-done.9), calls=%async_computation.4 | async-start | bytes 21495808 | tf_op jit(solution)/shard_map/all_to_all | solution.py:566
  72.3 113.3 %reduce-scatter.3.cloned.1.call-start = ((), (), s32[]{:S(2)}) async-start(), calls=%async_computation.7 | async-start | bytes 4718592 | tf_op jit(solution)/shard_map/reduce_scatter | solution.py:515
  78.0 179.6 %all-gather.8.cloned.1.call-start = ((), (), s32[]{:S(2)}) async-start(), calls=%async_computation.8 | async-start | bytes 4718592 | tf_op jit(solution)/shard_map/all_gather | solution.py:516
  185.6 135.8 %all-gather.10.cloned.1.call-start = ((), (), s32[]{:S(2)}) async-start(), calls=%async_computation.9 | async-start | bytes 2621440 | tf_op jit(solution)/shard_map/all_gather | solution.py:518
  201.8 56.8 %copy-start.32 = (s32[2,16,53]{2,1,0:T(8,128)}, s32[2,16,53]{2,1,0:T(8,128)S(1)}, u32[]{:S(2)}) copy-start(s32[2,16,53]{2,1,0:T(8,128)S(1)} %scatter.4) | copy-start | bytes 20356
  324.1 14.8 %collective-permute-start.15 = (f32[256,256]{0,1:T(8,128)S(1)}, f32[256,256]{0,1:T(8,128)}, u32[]{:S(2)}, u32[]{:S(2)}) collective-permute-start(f32[256,256]{0,1:T(8,128)S(1)} %fusion.34), channel_id=1, source_target_pairs={{0,24},{1,25},{2,26},{3,27},{4,28},{5,29},{6,30},{7,31}} | collective-permute-start | bytes 786440 | tf_op jit(solution)/shard_map/ppermute | solution.py:612
  325.5 16.8 %collective-permute-start.14 = (f32[256,256]{0,1:T(8,128)S(1)}, f32[256,256]{0,1:T(8,128)}, u32[]{:S(2)}, u32[]{:S(2)}) collective-permute-start(f32[256,256]{0,1:T(8,128)S(1)} %fusion.34), channel_id=1, source_target_pairs={{0,16},{1,17},{2,18},{3,19},{4,20},{5,21},{6,22},{7,23}} | collective-permute-start | bytes 786440 | tf_op jit(solution)/shard_map/ppermute | solution.py:612
  333.1 33.1 %collective-permute-start.16 = (f32[512,256]{1,0:T(8,128)S(1)}, f32[512,256]{1,0:T(8,128)S(1)}, u32[]{:S(2)}, u32[]{:S(2)}) collective-permute-start(f32[512,256]{1,0:T(8,128)S(1)} %bitcast.190), channel_id=1, source_target_pairs={{0,0},{1,2},{2,4},{3,6},{4,1},{5,3},{6,5},{7,7},{8,8},{9,10},{10,1... | collective-permute-start | bytes 1572872 | tf_op jit(solution)/shard_map/ppermute | solution.py:608
  333.8 32.4 %collective-permute-start.17 = (f32[512,256]{1,0:T(8,128)S(1)}, f32[512,256]{1,0:T(8,128)S(1)}, u32[]{:S(2)}, u32[]{:S(2)}) collective-permute-start(f32[512,256]{1,0:T(8,128)S(1)} %bitcast.189), channel_id=1, source_target_pairs={{0,2},{1,4},{2,6},{3,0},{4,3},{5,5},{6,7},{7,1},{8,10},{9,12},{10,... | collective-permute-start | bytes 1572872 | tf_op jit(solution)/shard_map/ppermute | solution.py:608
  338.8 27.4 %collective-permute-start.18 = (f32[512,256]{1,0:T(8,128)S(1)}, f32[512,256]{1,0:T(8,128)}, u32[]{:S(2)}, u32[]{:S(2)}) collective-permute-start(f32[512,256]{1,0:T(8,128)S(1)} %bitcast.188), channel_id=1, source_target_pairs={{0,4},{1,6},{2,0},{3,2},{4,5},{5,7},{6,1},{7,3},{8,12},{9,14},{10,... | collective-permute-start | bytes 1572872 | tf_op jit(solution)/shard_map/ppermute | solution.py:608
  338.9 27.3 %collective-permute-start.19 = (f32[512,256]{1,0:T(8,128)S(1)}, f32[512,256]{1,0:T(8,128)}, u32[]{:S(2)}, u32[]{:S(2)}) collective-permute-start(f32[512,256]{1,0:T(8,128)S(1)} %bitcast.187), channel_id=1, source_target_pairs={{0,6},{1,0},{2,2},{3,4},{4,7},{5,1},{6,3},{7,5},{8,14},{9,8},{10,1... | collective-permute-start | bytes 1572872 | tf_op jit(solution)/shard_map/ppermute | solution.py:608
  342.3 13.3 %collective-permute-start.13 = (f32[256,256]{0,1:T(8,128)S(1)}, f32[256,256]{0,1:T(8,128)}, u32[]{:S(2)}, u32[]{:S(2)}) collective-permute-start(f32[256,256]{0,1:T(8,128)S(1)} %fusion.34), channel_id=1, source_target_pairs={{0,8},{1,9},{2,10},{3,11},{4,12},{5,13},{6,14},{7,15}} | collective-permute-start | bytes 786440 | tf_op jit(solution)/shard_map/ppermute | solution.py:612
  343.7 22.6 %all-to-all-start.3 = ((s32[32,1,53]{2,1,0:T(1,128)}), s32[32,1,53]{2,1,0:T(1,128)S(1)}, u32[]{:S(2)}, u32[]{:S(2)}) async-start(s32[32,1,53]{2,1,0:T(1,128)} %bitcast.203), calls=%async_computation.5 | async-start | bytes 32768 | tf_op jit(solution)/shard_map/all_to_all | solution.py:624
  366.2 1.0 copy-start.24
  367.3 94.8 %all-to-all-start.4 = ((f32[16,52,8,128]{3,2,1,0:T(8,128)}), f32[16,52,8,128]{3,2,1,0:T(8,128)S(1)}, u32[]{:S(2)}, u32[]{:S(2)}) async-start(f32[16,52,8,128]{3,2,1,0:T(8,128)} %bitcast.47), calls=%async_computation.6 | async-start | bytes 6815744 | tf_op jit(solution)/shard_map/all_to_all | solution.py:647
  374.9 33.8 %copy-start.34 = (s32[2]{0:T(128)}, s32[2]{0:T(128)S(1)}, u32[]{:S(2)}) copy-start(s32[2]{0:T(128)S(1)} %pad_add_fusion.2.place_ref) | copy-start | bytes 28
  387.9 2.2 copy-start.7
  391.1 9.6 %copy-start.23 = (f32[512,256]{1,0:T(8,128)S(1)}, f32[512,256]{1,0:T(8,128)}, u32[]{:S(2)}) copy-start(f32[512,256]{1,0:T(8,128)} %copy-done.22) | copy-start | bytes 1572868
  391.1 9.6 %copy-start.25 = (f32[512,256]{1,0:T(8,128)S(1)}, f32[512,256]{1,0:T(8,128)}, u32[]{:S(2)}) copy-start(f32[512,256]{1,0:T(8,128)} %copy-done.24) | copy-start | bytes 1572868
  396.1 2.6 copy-start.10
  398.8 1.9 copy-start.11
  405.6 1.7 copy-start.12
  407.4 1.4 copy-start.14
  462.1 11.6 %copy-start.30 = (s32[128]{0:T(128)S(1)}, s32[128]{0:T(128)}, u32[]{:S(2)}) copy-start(s32[128]{0:T(128)} %valid_ref.1) | copy-start | bytes 1540
  (2 other events, 1.7 us)
Sparse Core Ops, SparseCore 0:
  78.1 107.4 reduce-scatter.2
  187.7 69.8 all-gather.7
  259.2 62.1 all-gather.9
